TPU v7x, 32 devices: a whole 2x2x4 slice. The times are simulated.
32 devices in a mesh: blk: 4 (over y, core), dp: 8 (over z, x).
Axes of the slice: x: 2, y: 2, z: 4, core: 2. Of those that a mesh axis runs over, the one named last changes fastest.
Arguments:
- inputs: bfloat16 [8, 1024, 512], P('dp', 'blk'), may hold values from -6 to 6
- segments: int32 [8, 1024], P('dp'), may hold values from 0 to 32, as said below
- attention_routes: int32 [2, 8, 1024, 4], P(None, 'dp', 'blk'), may hold values from 0 to 7, all different within a row
- expert_routes: int32 [2, 8, 1024, 2], P(None, 'dp', 'blk'), may hold values from 0 to 15, all different within a row; in each aligned block of 256 rows (0 to 255, 256 to 511, ..., all dimensions but the last counted through in order) at most 48 rows name the same one
- gain_mixer: bfloat16 [512], replicated, may hold values from 0.5 to 1.5
- gain_expert: bfloat16 [512], replicated, may hold values from 0.5 to 1.5
- weight_query: bfloat16 [8, 512, 512], P(None, 'dp', 'blk'), may hold values from -0.25 to 0.25
- weight_key: bfloat16 [512, 512], P('dp', 'blk'), may hold values from -0.25 to 0.25
- weight_value: bfloat16 [512, 512], P('dp', 'blk'), may hold values from -0.25 to 0.25
- weight_out: bfloat16 [8, 512, 512], P(None, 'blk', 'dp'), may hold values from -2 to 2
- router_mixer: bfloat16 [512, 8], replicated, may hold values from -0.125 to 0.125
- router_expert: bfloat16 [512, 16], replicated, may hold values from -0.1875 to 0.1875
- weight_in: bfloat16 [16, 512, 2048], P('dp', 'blk'), may hold values from -0.25 to 0.25
- weight_back: bfloat16 [16, 2048, 512], P('dp', 'blk'), may hold values from -0.125 to 0.125
- halt_weight: bfloat16 [512], replicated, may hold values from -0.25 to 0.25
- cotangent: bfloat16 [8, 1024, 512], P('dp', 'blk'), may hold values from -6 to 6
Outputs:
- result: bfloat16 [8, 1024, 512], P('dp', 'blk')
- input_grad: bfloat16 [8, 1024, 512], P('dp', 'blk')
- gain_mixer_grad: float32 [512], replicated
- gain_expert_grad: float32 [512], replicated
- query_grad: float32 [8, 512, 512], P(None, 'dp', 'blk')
- key_grad: float32 [512, 512], P('dp', 'blk')
- value_grad: float32 [512, 512], P('dp', 'blk')
- out_grad: float32 [8, 512, 512], P(None, 'blk', 'dp')
- router_mixer_grad: float32 [512, 8], replicated
- router_expert_grad: float32 [512, 16], replicated
- in_grad: float32 [16, 512, 2048], P('dp', 'blk')
- back_grad: float32 [16, 2048, 512], P('dp', 'blk')
- halt_grad: float32 [512], replicated
Inputs may be any that keep to these rules, and one draw needn't show every extreme that they name: `segments`: each pack is cut into sentences along its positions: a first one of 1 to b - 1 positions, then sentences of exactly b positions, the last one possibly shorter, where the pack's bucket length b is 256, 128, 64 or 32; pack 0 has b = 256 and the last pack b = 32. No sentence begins at a multiple of 256. Ids number the sentences of a pack from 0 in order. `attention_routes`: each position names 4 different attention experts. `expert_routes`: each position names 2 different experts. In each aligned block of 256 positions of one step and pack, no expert is named by more than 48 positions; some expert is named by exactly 48 in some blocks.
All inputs are finite; a program needn't handle non-finite values.
Results may differ from a plain program's by a relative error of at most 0.024.
Values may be sent and summed in bfloat16 or wider, within the bound.
A program may use at most 256 MiB of HBM per device.

v0:
```python
import functools
from types import SimpleNamespace
from typing import NamedTuple

import jax
import jax.numpy as jnp
from jax import lax
from jax.experimental import pallas as pl
from jax.experimental.pallas import tpu as pltpu
from jax.sharding import PartitionSpec as P

HEADS = 8
HD = 64
MAXLEN = 256
QROWS = 128
WINDOW = MAXLEN + QROWS
LANES = 128
EPSILON = 1e-06
MASKED_SCORE = -1e30
MESH = pl.DeviceIdType.MESH
BF = jnp.bfloat16
F32 = jnp.float32
VMEM_BYTES = 61 * 2**20


class Plan(NamedTuple):
    blk: int
    dp: int
    lo: int
    hi: int
    seq: int
    width: int
    heads: int
    mixers: int
    top: int
    experts: int
    local: int
    group: int
    cap: int
    ff: int

    @property
    def length(self):
        return self.blk * self.seq

    @property
    def cols(self):
        return self.heads * HD

    @property
    def qkv(self):
        return (self.mixers + 2) * self.cols

    @property
    def all_cols(self):
        return (2 * self.mixers + 2) * self.cols

    @property
    def blocks(self):
        return self.length // QROWS

    @property
    def slots(self):
        return self.experts * self.cap

    @property
    def head_cols(self):
        return (self.mixers + 2) * HD

    @property
    def parts(self):
        heads = [slice(h * self.head_cols, (h + 1) * self.head_cols) for h in range(self.heads)]
        return (*heads, slice(self.qkv, self.all_cols))

    @property
    def tile(self):
        return 512 if self.slots <= 768 else 256

    @property
    def chips(self):
        return self.blk // 2


def mm(a, b):
    return lax.dot_general(a, b, (((1,), (0,)), ((), ())), preferred_element_type=F32)


def mm_nt(a, b):
    return lax.dot_general(a, b, (((1,), (1,)), ((), ())), preferred_element_type=F32)


def place():
    return lax.axis_index("blk"), lax.axis_index("dp")


def turn(index, by, size):
    return lax.rem(index + (by % size), size)


def greet(peers):
    barrier = pltpu.get_barrier_semaphore()
    for peer in peers:
        pl.semaphore_signal(barrier, inc=1, device_id=peer, device_id_type=MESH)


def answered(peers):
    pl.semaphore_wait(pltpu.get_barrier_semaphore(), len(peers))


def send(src, dst, sems, slot, peer):
    copy = pltpu.make_async_remote_copy(
        src_ref=src,
        dst_ref=dst,
        send_sem=sems[0].at[slot],
        recv_sem=sems[1].at[slot],
        device_id=peer,
        device_id_type=MESH,
    )
    copy.start()
    return copy


def aligned(value, by):
    return pl.multiple_of(value, by)


def pack_peers(p):
    b, d = place()
    y, c = b // 2, lax.rem(b, 2)
    peers = [(2 * y + 1 - c, d)]
    return peers + [(2 * turn(y, s, p.chips) + c, d) for s in range(1, p.chips)]


def slot_peer(p, s):
    b, d = place()
    e, g = b // p.group, lax.rem(b, p.group)
    return (turn(e, s // p.dp, p.local) * p.group + g, turn(d, s % p.dp, p.dp))


def slot_peers(p):
    return [slot_peer(p, s) for s in range(1, p.experts)]


def slot_source(p, s):
    b, d = place()
    e, g = b // p.group, lax.rem(b, p.group)
    return (turn(e, -(s // p.dp), p.local) * p.group + g, turn(d, -(s % p.dp), p.dp))


def dp_peers(p):
    b, d = place()
    z, x = d // p.lo, lax.rem(d, p.lo)
    peers = [(b, turn(z, s, p.hi) * p.lo + x) for s in range(1, p.hi)]
    return peers + [(b, z * p.lo + turn(x, t, p.lo)) for t in range(1, p.lo)]


def expert_peers(p):
    b, d = place()
    e, g = b // p.group, lax.rem(b, p.group)
    peers = [(turn(e, s, p.local) * p.group + g, d) for s in range(1, p.local)]
    return peers + [(e * p.group + turn(g, t, p.group), d) for t in range(1, p.group)]


def link(src, dst, sems, slot, peer):
    return pltpu.make_async_remote_copy(
        src_ref=src,
        dst_ref=dst,
        send_sem=sems[0].at[slot],
        recv_sem=sems[1].at[slot],
        device_id=peer,
        device_id_type=MESH,
    )


class PackGather:
    def __init__(self, p, buf, sems):
        self.p, self.buf, self.far, self.near = p, buf, sems[0:2], sems[2:4]
        self.done_near = self.done_far = False

    def begin(self):
        p = self.p
        b, d = place()
        y, c = b // 2, lax.rem(b, 2)
        own = self.buf.at[b]
        self.first = [
            send(own, own, self.far, s - 1, (2 * turn(y, s, p.chips) + c, d))
            for s in range(1, p.chips)
        ]
        self.second = [send(own, own, self.near, 0, (2 * y + 1 - c, d))]

    def finish_near(self):
        if not self.done_near:
            self.second[0].wait_recv()
        self.done_near = True

    def finish_far(self):
        if self.done_far:
            return
        self.done_far = True
        p = self.p
        b, d = place()
        y, c = b // 2, lax.rem(b, 2)
        for s in range(1, p.chips):
            self.first[s - 1].wait_recv()
            block = self.buf.at[2 * turn(y, -s, p.chips) + c]
            self.second.append(send(block, block, self.near, s, (2 * y + 1 - c, d)))
        self.finish_near()
        for copy in self.second[1:]:
            copy.wait_recv()

    def end(self):
        for copy in self.first + self.second:
            copy.wait_send()


class PackSum:
    def __init__(self, p, bufs, sems):
        self.p, self.bufs = p, bufs
        self.far, self.near = sems[0:2], sems[2:4]
        self.first, self.second = {}, []

    def give(self, s, term):
        p, r = self.p, self.bufs
        b, d = place()
        y, c = b // 2, lax.rem(b, 2)
        r.part[s] = term.astype(BF)
        self.first[s] = send(r.part.at[s], r.near_in.at[s], self.near, s, (2 * y + 1 - c, d))

    def pass_on(self, s, term):
        p, r = self.p, self.bufs
        b, d = place()
        y, c = b // 2, lax.rem(b, 2)
        self.first[s].wait_recv()
        r.far_out[s - 1] = (term + r.near_in[s].astype(F32)).astype(BF)
        self.second.append(
            send(r.far_out.at[s - 1], r.far_in.at[s - 1], self.far, s - 1, (2 * turn(y, s, p.chips) + c, d))
        )

    def total(self, term):
        r = self.bufs
        self.first[0].wait_recv()
        term = term + r.near_in[0].astype(F32)
        for k, copy in enumerate(self.second):
            copy.wait_recv()
            term = term + r.far_in[k].astype(F32)
        for copy in list(self.first.values()) + self.second:
            copy.wait_send()
        return term


def slot_send(p, src, dst, sems, s, peer):
    rows = pl.ds(s * p.cap, p.cap)
    return send(src.at[rows], dst.at[rows], sems, s, peer)


def slot_sends(p, src, dst, sems, peer):
    dst[0 : p.cap, :] = src[0 : p.cap, :]
    return {s: slot_send(p, src, dst, sems, s, peer(p, s)) for s in range(1, p.experts)}


def receive(copies, sources):
    for s in sources:
        if s in copies:
            copies[s].wait_recv()


def sent(copies):
    for copy in copies.values() if isinstance(copies, dict) else copies:
        copy.wait_send()


def move(r, src, dst):
    copy = pltpu.make_async_copy(src, dst, r.moves.at[r.moved])
    r.moved += 1
    copy.start()
    return copy


def moves(r, pairs):
    return [move(r, src, dst) for src, dst in pairs]


def arrive(copies):
    for copy in copies:
        copy.wait()
    copies.clear()


def norm_parts(state):
    inverse = lax.rsqrt(jnp.mean(state * state, axis=-1, keepdims=True) + EPSILON)
    return inverse, state * inverse


def norm_back(state, gain, grad):
    inverse, unit = norm_parts(state)
    scaled = grad * gain
    back = inverse * scaled - state * (inverse * inverse * inverse) * jnp.mean(
        scaled * state, axis=-1, keepdims=True
    )
    return back, jnp.sum(grad * unit, axis=0, keepdims=True)


def segment_columns(p, segments, seg_cols):
    seg_cols[0:MAXLEN, :] = jnp.full((MAXLEN, 8), -1.0, F32)
    for start in range(0, p.length, QROWS):
        row = segments[:, start : start + QROWS].astype(F32)
        seg_cols[MAXLEN + start : MAXLEN + start + QROWS, :] = jnp.broadcast_to(row, (8, QROWS)).T


def attention_mask(r, start):
    keys = r.seg_cols[pl.ds(start, WINDOW), 0:1]
    queries = r.segments[:, pl.ds(start, QROWS)].astype(F32)
    key_at = lax.broadcasted_iota(jnp.int32, (WINDOW, QROWS), 0) - MAXLEN
    query_at = lax.broadcasted_iota(jnp.int32, (WINDOW, QROWS), 1)
    return jnp.where((key_at <= query_at) & (keys == queries), 0.0, MASKED_SCORE)


def pick_rows(p, routes, terms):
    picked = []
    for j in range(p.top):
        row = routes[j : j + 1, :]
        total = None
        for e in range(p.mixers):
            term = jnp.where(row == e, terms(e), 0.0)
            total = term if total is None else total + term
        picked.append(total)
    return picked


def spread_rows(p, routes, values, e):
    total = None
    for j in range(p.top):
        term = jnp.where(routes[j : j + 1, :] == e, values[j], 0.0)
        total = term if total is None else total + term
    return total


def pick_table(p, r, step, bb):
    return r.all_picks[bb, 8 * step : 8 * step + p.top, :]


def transposed(dst, src, first, start, stop, tile):
    for at in range(0, stop - start, tile):
        piece = src[:, start + at : start + at + tile]
        dst[first + at : first + at + tile, :] = piece.astype(F32).T.astype(BF)


def project_rows(p, r, head):
    start, stop = head * p.head_cols, (head + 1) * p.head_cols
    transposed(r.w_t, r.all_w, start, start, stop, LANES)


def project_gates(p, r, a, step, bb):
    table = pick_table(p, r, step, bb)
    logits = mm(r.router_row[...], a.nt[bb])
    chosen = pick_rows(p, table, lambda e: logits[e : e + 1, :])
    peak = functools.reduce(jnp.maximum, chosen)
    chosen = [jnp.exp(row - peak) for row in chosen]
    scale = 1.0 / sum(chosen)
    for j in range(p.top):
        a.gates[bb, j : j + 1, :] = chosen[j] * scale


def project(p, r, a, step, bb, head):
    sub = p.seq // QROWS
    if head == 0:
        project_gates(p, r, a, step, bb)
    table = pick_table(p, r, step, bb)
    values = mm(r.w_t[head * p.head_cols : (head + 1) * p.head_cols, :], a.nt[bb])
    for k in range(sub):
        lanes = slice(k * QROWS, (k + 1) * QROWS)
        queries = pick_rows(p, table[:, lanes], lambda e: values[e * HD : (e + 1) * HD, lanes])
        for j in range(p.top):
            a.qs[head, bb * sub + k, :, j * QROWS : (j + 1) * QROWS] = (queries[j] * (HD**-0.5)).astype(BF)
    at = pl.ds(aligned(MAXLEN + bb * p.seq, QROWS), p.seq)
    keys = values[p.mixers * HD : (p.mixers + 1) * HD, :]
    a.kt[head, :, at] = keys.astype(BF)
    a.vt[head, :, at] = values[(p.mixers + 1) * HD :, :].astype(BF)
    r.k_rows[head, at, :] = keys.T.astype(BF)


def attend(p, r, a, step, bb, head):
    sub = p.seq // QROWS
    for k in range(sub):
        i = bb * sub + k
        start = aligned(i * QROWS, QROWS)
        keys = pl.ds(start, WINDOW)
        bias = attention_mask(r, start)
        bias = jnp.concatenate([bias] * p.top, axis=1)
        scores = mm(r.k_rows[head, keys, :], a.qs[head, i]) + bias
        peak = jnp.max(scores, axis=0, keepdims=True)
        scores = jnp.exp(scores - peak)
        total = jnp.sum(scores, axis=0, keepdims=True)
        a.lse[i, head : head + 1, :] = peak + jnp.log(total)
        probs = (scores * (1.0 / total)).astype(BF)
        past = mm(a.vt[head, :, keys], probs)
        a.att[head, i] = past.astype(BF)
        at = pl.ds(k * QROWS, QROWS)
        table = r.all_picks[bb, 8 * step : 8 * step + p.top, at]
        weights = a.gates[bb, 0 : p.top, at]
        values = [past[:, j * QROWS : (j + 1) * QROWS] * weights[j : j + 1, :] for j in range(p.top)]
        for e in range(p.mixers):
            rows = slice(e * p.cols + head * HD, e * p.cols + (head + 1) * HD)
            a.mix[rows, pl.ds(start, QROWS)] = spread_rows(p, table, values, e).astype(BF)


def each_block(work, first, count):
    @pl.loop(0, count)
    def _(k):
        work(first + k)


def attention_forward(p, r, a, step, state, before, ready, tick, out_ready, after):
    b, _ = place()
    y, c = b // 2, lax.rem(b, 2)
    a.nt[b] = (norm_parts(state)[1] * r.gain_one[...].astype(F32)).T.astype(BF)
    gather = PackGather(p, a.nt, a.gather_sems)
    gather.begin()
    r.k_rows[:, 0:MAXLEN, :] = jnp.zeros((p.heads, MAXLEN, HD), BF)
    a.kt[:, :, 0:MAXLEN] = jnp.zeros((p.heads, HD, MAXLEN), BF)
    a.vt[:, :, 0:MAXLEN] = jnp.zeros((p.heads, HD, MAXLEN), BF)
    before(gather)
    shares = PackSum(p, r, a.sum_sems)

    def branch(bb):
        return mm(r.all_w[:, p.qkv :], a.mix[:, pl.ds(aligned(bb * p.seq, p.seq), p.seq)])

    for head in range(p.heads):
        if head == 0:
            project(p, r, a, step, b, head)
            gather.finish_near()
            project(p, r, a, step, 2 * y + 1 - c, head)
            tick()
            attend(p, r, a, step, 2 * y + 1, head)
            gather.finish_far()
            tick()
            for s in range(1, p.chips):
                each_block(lambda bb: project(p, r, a, step, bb, 0), 2 * turn(y, s, p.chips), 2)
            tick()
        else:
            ready(head)
            each_block(lambda bb: project(p, r, a, step, bb, head), 0, p.blk)
            attend(p, r, a, step, 2 * y + 1, head)
            tick()
        for s in range(1, p.chips):
            yy = turn(y, s, p.chips)
            attend(p, r, a, step, 2 * yy + 1 - c, head)
            tick()
            if head == p.heads - 1:
                if s == 1:
                    out_ready()
                shares.give(s, branch(2 * yy + 1 - c))
            attend(p, r, a, step, 2 * yy + c, head)
            tick()
            if head == p.heads - 1:
                shares.pass_on(s, branch(2 * yy + c))
        if head == p.heads - 1:
            after()
        attend(p, r, a, step, 2 * y, head)
        tick()
    shares.give(0, branch(2 * y + 1 - c))
    total = shares.total(branch(b))
    gather.end()
    return total


def attention_grads(p, r, a, step, bb):
    sub = p.seq // QROWS
    table = pick_table(p, r, step, bb)
    weights = a.gates[bb, 0 : p.top, :]
    values = mm(r.wo[...], r.gt[bb])
    for k in range(sub):
        lanes = slice(k * QROWS, (k + 1) * QROWS)
        here = table[:, lanes]
        grads = [None] * p.top
        for head in range(p.heads):
            picked = pick_rows(
                p, here, lambda e: values[e * p.cols + head * HD : e * p.cols + (head + 1) * HD, lanes]
            )
            for j in range(p.top):
                slot = slice(j * QROWS, (j + 1) * QROWS)
                past = a.att[head, bb * sub + k, :, slot].astype(F32)
                dot = jnp.sum(picked[j] * past, axis=0, keepdims=True)
                grads[j] = dot if head == 0 else grads[j] + dot
                gate = weights[j : j + 1, lanes]
                r.means[bb * sub + k, head : head + 1, slot] = dot * gate
                a.att[head, bb * sub + k, :, slot] = (picked[j] * gate).astype(BF)
        mean = sum(weights[j : j + 1, lanes] * grads[j] for j in range(p.top))
        back = [weights[j : j + 1, lanes] * (grads[j] - mean) for j in range(p.top)]
        for e in range(p.mixers):
            r.dlog[bb, e : e + 1, lanes] = spread_rows(p, here, back, e)


def probs_at(p, i, head):
    across = p.ff // (p.top * QROWS)
    each = p.slots // WINDOW * across
    unit = i * p.heads + head
    rows = aligned(lax.rem(unit, each) // across * WINDOW, QROWS)
    lanes = aligned(lax.rem(unit, across) * (p.top * QROWS), QROWS)
    return unit // each, pl.ds(rows, WINDOW), pl.ds(lanes, p.top * QROWS)


def attention_probs(p, r, a):
    @pl.loop(0, p.blocks)
    def _(i):
        start = aligned(i * QROWS, QROWS)
        bias = attention_mask(r, start)
        bias = jnp.concatenate([bias] * p.top, axis=1)
        for head in range(p.heads):
            scores = mm(r.k_rows[head, pl.ds(start, WINDOW), :], a.qs[head, i]) + bias
            plane, rows, lanes = probs_at(p, i, head)
            r.keep[plane, rows, lanes] = jnp.exp(scores - a.lse[i, head : head + 1, :]).astype(BF)


def attention_rows(p, r, a, keys):
    @pl.loop(0, (p.length + MAXLEN) // QROWS)
    def _(k):
        at = pl.ds(aligned(k * QROWS, QROWS), QROWS)
        for head in range(p.heads):
            r.v_rows[head, at, :] = a.vt[head, :, at].astype(F32).T.astype(BF)
            if keys:
                r.k_rows[head, at, :] = a.kt[head, :, at].astype(F32).T.astype(BF)


def attend_back(p, r, a, step, bb, head):
    sub = p.seq // QROWS
    for k in range(sub):
        i = bb * sub + k
        start = aligned(i * QROWS, QROWS)
        keys = pl.ds(start, WINDOW)
        plane, rows, lanes = probs_at(p, i, head)
        probs = r.keep[plane, rows, lanes]
        grads = a.att[head, i]
        mean = r.means[i, head : head + 1, :]
        dscores = (probs.astype(F32) * (mm(r.v_rows[head, keys, :], grads) - mean)).astype(BF)
        r.dvt[head, :, keys] += mm_nt(grads, probs)
        r.dkt[head, :, keys] += mm_nt(a.qs[head, i], dscores)
        merged = mm(a.kt[head, :, keys], dscores) * (HD**-0.5)
        at = pl.ds(k * QROWS, QROWS)
        table = r.all_picks[bb, 8 * step : 8 * step + p.top, at]
        values = [merged[:, j * QROWS : (j + 1) * QROWS] for j in range(p.top)]
        for e in range(p.mixers):
            first = head * p.head_cols + e * HD
            r.dall[first : first + HD, pl.ds(start, QROWS)] = spread_rows(p, table, values, e).astype(BF)


def attention_backward(p, r, a, step, state, grad, before, middle, head_done):
    b, _ = place()
    y, c = b // 2, lax.rem(b, 2)
    r.gt[b] = grad.T.astype(BF)
    gather = PackGather(p, r.gt, a.back_gather_sems)
    gather.begin()
    r.dkt[...] = jnp.zeros_like(r.dkt)
    r.dvt[...] = jnp.zeros_like(r.dvt)
    before()
    router_col = r.router_row[...].astype(F32).T.astype(BF)

    def key_value_grads(lanes, past):
        for head in range(p.heads):
            first = head * p.head_cols + p.mixers * HD
            r.dall[first : first + HD, lanes] = r.dkt[head, :, past].astype(BF)
            r.dall[first + HD : first + 2 * HD, lanes] = r.dvt[head, :, past].astype(BF)

    def branch(bb):
        lanes = pl.ds(aligned(bb * p.seq, p.seq), p.seq)
        key_value_grads(lanes, pl.ds(aligned(bb * p.seq + MAXLEN, QROWS), p.seq))
        return mm(r.all_w[:, : p.qkv], r.dall[:, lanes]) + mm(router_col, r.dlog[bb].astype(BF))

    shares = PackSum(p, r, a.back_sum_sems)
    for head in range(p.heads):
        if head == 0:
            attention_grads(p, r, a, step, b)
            gather.finish_near()
            attention_grads(p, r, a, step, 2 * y + 1 - c)
            attend_back(p, r, a, step, 2 * y, head)
            gather.finish_far()
            for s in range(1, p.chips):
                each_block(lambda bb: attention_grads(p, r, a, step, bb), 2 * turn(y, s, p.chips), 2)
            middle()
        else:
            attend_back(p, r, a, step, 2 * y, head)
        for s in range(1, p.chips):
            each_block(lambda bb: attend_back(p, r, a, step, bb, head), 2 * turn(y, s, p.chips), 2)
        if head == p.heads - 1:
            for s in range(1, p.chips):
                yy = turn(y, s, p.chips)
                shares.give(s, branch(2 * yy + 1 - c))
                shares.pass_on(s, branch(2 * yy + c))
        attend_back(p, r, a, step, 2 * y + 1, head)
        if head < p.heads - 1:
            key_value_grads(slice(0, p.length), slice(MAXLEN, MAXLEN + p.length))
            head_done(head)
    shares.give(0, branch(2 * y + 1 - c))
    own = branch(b)
    head_done(p.heads - 1)
    router = sum(mm_nt(r.dlog[bb].astype(BF), a.nt[bb]) for bb in range(p.blk))
    grad_n = shares.total(own).T
    gather.end()
    back, gain = norm_back(state, r.gain_one[...].astype(F32), grad_n)
    return grad + back, gain, router


def attention_weight_grads(p, r, a, start, stop, add):
    for first in range(start, stop, 2 * LANES):
        tile = min(2 * LANES, stop - first)
        total = None
        for bb in range(p.blk):
            lanes = slice(bb * p.seq, (bb + 1) * p.seq)
            if first < p.qkv:
                term = mm_nt(a.nt[bb], r.dall[first : first + tile, lanes])
            else:
                term = mm_nt(r.gt[bb], a.mix[first - p.qkv : first - p.qkv + tile, lanes])
            total = term if total is None else total + term
        at = slice(first, first + tile)
        r.grad_w[:, at] = (r.grad_w[:, at].astype(F32) + total if add else total).astype(BF)


def own_lane(p):
    b, d = place()
    mine = d * p.local + b // p.group
    return jnp.where(lax.broadcasted_iota(jnp.int32, (1, LANES), 1) == mine, 1.0, 0.0)


def slot_gates(p, r, rows, pair):
    own = own_lane(p)
    logits = mm_nt(rows, r.router[...])
    return 1.0 / (1.0 + jnp.exp(jnp.sum(logits * (pair - 2.0 * own), axis=-1, keepdims=True)))


def gelu_both(inner):
    half = 0.5 * (1.0 + lax.erf(inner * 0.7071067811865476))
    slope = half + inner * jnp.exp(-0.5 * inner * inner) * 0.3989422804014327
    return inner * half, slope


def fill_router(p, r):
    r.router[...] = jnp.zeros_like(r.router)
    r.router[0 : p.experts, :] = r.router_in[...]


def slot_groups(p):
    per = max(1, p.experts // 4)
    return [(pl.ds(first * p.cap, per * p.cap), range(first, first + per)) for first in range(0, p.experts, per)]


def expert_output(p, r, rows, at, keep):
    total = None
    for start in range(0, p.ff, p.tile):
        lanes = slice(start, start + p.tile)
        inner = mm(rows, r.all_in[:, lanes])
        if keep:
            act, slope = gelu_both(inner)
            act = act.astype(BF)
            r.keep[0, at, lanes] = act
            r.keep[1, at, lanes] = slope.astype(BF)
        else:
            act = (inner * (0.5 * (1.0 + lax.erf(inner * 0.7071067811865476)))).astype(BF)
        term = mm(act, r.all_back[lanes, :])
        total = term if total is None else total + term
    return total


def expert_keep(p, r, rows, at):
    for start in range(0, p.ff, p.tile):
        lanes = slice(start, start + p.tile)
        act, slope = gelu_both(mm(rows, r.all_in[:, lanes]))
        r.keep[0, at, lanes] = act.astype(BF)
        r.keep[1, at, lanes] = slope.astype(BF)


def expert_input_grad(p, r, at, u, rows, out, pair, dst):
    gate = slot_gates(p, r, rows, pair)
    grads = (u * gate).astype(BF)
    r.u_in[at, :] = grads
    coeff = gate * (1.0 - gate) * jnp.sum(u * out, axis=-1, keepdims=True) * (2.0 * own_lane(p) - pair)
    coeff = coeff.astype(BF)
    r.coeff[at, :] = coeff
    dst[at, :] = mm(coeff, r.router[...]).astype(BF)
    total = None
    for start in range(0, p.ff, p.tile):
        lanes = slice(start, start + p.tile)
        inner = (mm_nt(grads, r.all_back[lanes, :]) * r.keep[1, at, lanes].astype(F32)).astype(BF)
        r.keep[1, at, lanes] = inner
        term = mm_nt(inner, r.all_in[:, lanes])
        total = term if total is None else total + term
    dst[at, :] = (total + dst[at, :].astype(F32)).astype(BF)


def expert_weight_grads(p, r, arrived, add):
    r.arrived_t[...] = arrived[...].astype(F32).T.astype(BF)
    for start in range(0, p.ff, p.tile // 2):
        lanes = slice(start, start + p.tile // 2)
        term = mm(r.keep[0, :, lanes].astype(F32).T.astype(BF), r.u_in[...])
        r.grad_back[lanes, :] = (r.grad_back[lanes, :].astype(F32) + term if add else term).astype(BF)
        term = mm(r.arrived_t[...], r.keep[1, :, lanes])
        r.grad_in[:, lanes] = (r.grad_in[:, lanes].astype(F32) + term if add else term).astype(BF)
    return mm(r.coeff[...].astype(F32).T.astype(BF)[0 : p.experts], arrived[...])


def slot_tables(p, r):
    b, d = place()
    e = b // p.group
    place_in = lax.broadcasted_iota(jnp.int32, (p.experts, 1), 0)
    ids = lax.rem(d + lax.rem(place_in, p.dp), p.dp) * p.local + lax.rem(e + place_in // p.dp, p.local)
    earlier = (
        lax.broadcasted_iota(jnp.int32, (p.seq, p.seq), 0) < lax.broadcasted_iota(jnp.int32, (p.seq, p.seq), 1)
    ).astype(BF)
    slot_ids = lax.broadcasted_iota(jnp.int32, (p.cap, p.seq), 0).astype(F32)
    r.pair_out[...] = jnp.zeros_like(r.pair_out)
    for step in range(2):
        one = r.routes[8 * step + p.top : 8 * step + p.top + 1, :]
        two = r.routes[8 * step + p.top + 1 : 8 * step + p.top + 2, :]
        member = jnp.where((one == ids) | (two == ids), 1.0, 0.0)
        rank = jnp.where(member > 0.5, mm(member.astype(BF), earlier), -1.0)
        both = jnp.broadcast_to((one + two).astype(F32), (8, p.seq)).astype(BF)
        for s in range(p.experts):
            table = jnp.where(rank[s : s + 1, :] == slot_ids, 1.0, 0.0).astype(BF)
            r.disp[step, pl.ds(s * p.cap, p.cap), :] = table
            r.pair_out[s, step : step + 1, 0 : p.cap] = mm_nt(both, table)[0:1]
        r.comb[step] = r.disp[step].astype(F32).T.astype(BF)
    r.pair_in[0] = r.pair_out[0]
    return [
        send(r.pair_out.at[s], r.pair_in.at[s], (r.pair_s, r.pair_r), s, slot_peer(p, s)) for s in range(1, p.experts)
    ]


def slot_pairs(p, r):
    b, d = place()
    mine = (d * p.local + b // p.group).astype(F32)
    lanes = lax.broadcasted_iota(jnp.int32, (p.cap, LANES), 1).astype(F32)
    for step in range(2):
        totals = r.pair_in[:, step, :].T
        for s in range(p.experts):
            other = totals[0 : p.cap, s : s + 1] - mine
            both = jnp.where(lanes == mine, 1.0, 0.0) + jnp.where(lanes == other, 1.0, 0.0)
            r.pair[step, pl.ds(s * p.cap, p.cap), :] = both.astype(BF)


def forward_kernel(p, r):
    b, d = place()
    z, x = d // p.lo, lax.rem(d, p.lo)
    e, g = b // p.group, lax.rem(b, p.group)
    own_rows = r.weight_key.shape[0]
    in_rows, back_rows = r.weight_in.shape[1], r.weight_back.shape[1]

    def w_at(index, part):
        return r.all_w.at[pl.ds(aligned(index * own_rows, own_rows), own_rows), p.parts[part]]

    def in_at(index):
        return r.all_in.at[pl.ds(aligned(index * in_rows, in_rows), in_rows)]

    def back_at(index):
        return r.all_back.at[pl.ds(aligned(index * back_rows, back_rows), back_rows)]

    peers = pack_peers(p) + slot_peers(p) + dp_peers(p) + expert_peers(p)
    greet(peers)
    own = pl.ds(aligned(d * own_rows, own_rows), own_rows)
    for head in range(p.heads):
        mine = slice(head * HD, (head + 1) * HD)
        shares = [r.weight_query[k, :, mine] for k in range(p.mixers)]
        shares += [r.weight_key[:, mine], r.weight_value[:, mine]]
        r.all_w[own, p.parts[head]] = jnp.concatenate(shares, axis=1)
    for k in range(p.mixers):
        r.all_w[own, p.qkv + k * p.cols : p.qkv + (k + 1) * p.cols] = r.weight_out[k]
    fill_router(p, r)
    segment_columns(p, r.segments, r.seg_cols)
    answered(peers)
    last = p.hi - 1

    def hop(part, k, up):
        rows = w_at((z - k if up else z + k) * p.lo + x, part)
        slot = (2 * part + (0 if up else 1)) * last + k
        return link(rows, rows, (r.hi_s, r.hi_r), slot, (b, (z + 1 if up else z - 1) * p.lo + x))

    def arrival(part, k, up):
        rows = w_at((z - 1 - k if up else z + 1 + k) * p.lo + x, part)
        return link(rows, rows, (r.hi_s, r.hi_r), (2 * part + (0 if up else 1)) * last + k, (b, d))

    def cross(part, source, t):
        rows = w_at(source * p.lo + x, part)
        slot = (part * p.hi + source) * (p.lo - 1) + t - 1
        return link(rows, rows, (r.lo_s, r.lo_r), slot, (b, z * p.lo + turn(x, t, p.lo)))

    def goes(k, up):
        return (z >= k) & (z < last) if up else (z + k <= last) & (z > 0)

    def comes(k, up):
        return z >= k + 1 if up else z + k + 1 <= last

    def w_begin(part):
        for up in (True, False):
            pl.when(goes(0, up))(lambda: hop(part, 0, up).start())
        for t in range(1, p.lo):
            cross(part, z, t).start()

    def w_pass(part, k):
        for up in (True, False):

            @pl.when(comes(k, up))
            def _():
                arrival(part, k, up).wait_recv()
                if k + 1 < last:
                    pl.when(goes(k + 1, up))(lambda: hop(part, k + 1, up).start())
                for t in range(1, p.lo):
                    cross(part, z - 1 - k if up else z + 1 + k, t).start()

    def w_finish(part):
        for source in range(p.hi):
            for t in range(1, p.lo):
                rows = w_at(source * p.lo + turn(x, -t, p.lo), part)
                slot = (part * p.hi + source) * (p.lo - 1) + t - 1
                link(rows, rows, (r.lo_s, r.lo_r), slot, (b, d)).wait_recv()

    def w_end():
        for part in range(p.heads + 1):
            for k in range(last):
                for up in (True, False):
                    pl.when(goes(k, up))(lambda: hop(part, k, up).wait_send())
            for source in range(p.hi):
                for t in range(1, p.lo):
                    cross(part, source, t).wait_send()

    local, over, beside = [], {}, []

    def experts_begin():
        for s in range(1, p.local):
            to = turn(e, s, p.local)
            peer = (to * p.group + g, d)
            over[s, 0] = send(r.weight_in.at[to], in_at(b), (r.wide_s, r.wide_r), 2 * s - 2, peer)
            over[s, 1] = send(r.weight_back.at[to], back_at(b), (r.wide_s, r.wide_r), 2 * s - 1, peer)
        for t in range(1, p.group):
            peer = (e * p.group + turn(g, t, p.group), d)
            beside.append(send(r.weight_in.at[e], in_at(b), (r.near_s, r.near_r), 2 * t - 2, peer))
            beside.append(send(r.weight_back.at[e], back_at(b), (r.near_s, r.near_r), 2 * t - 1, peer))

    def experts_pass():
        for s in range(1, p.local):
            source = turn(e, -s, p.local) * p.group + g
            for which, rows in ((0, in_at(source)), (1, back_at(source))):
                over[s, which].wait_recv()
                for t in range(1, p.group):
                    k = (s * (p.group - 1) + t - 1) * 2 + which
                    peer = (e * p.group + turn(g, t, p.group), d)
                    beside.append(send(rows, rows, (r.near_s, r.near_r), k, peer))

    tables = []
    saves = []

    w_begin(0)
    for step in range(2):
        r.routes[8 * step : 8 * step + p.top, :] = r.attention_routes[step]
        r.routes[8 * step + p.top : 8 * step + 6, :] = r.expert_routes[step]
        r.routes[8 * step + 6 : 8 * step + 8, :] = jnp.zeros((2, p.seq), jnp.int32)
    r.all_picks[b] = r.routes[...]
    picks = PackGather(p, r.all_picks, r.picks_sems)
    picks.begin()
    state = r.x[...].astype(F32)

    def before(gather):
        local.extend(moves(r, [(r.weight_in.at[e], in_at(b)), (r.weight_back.at[e], back_at(b))]))
        tables.extend(slot_tables(p, r))
        w_pass(0, 0)
        w_pass(0, 1)
        gather.finish_far()
        picks.finish_far()
        experts_begin()
        for k in range(2, last):
            w_pass(0, k)
        w_begin(1)
        w_finish(0)
        project_rows(p, r, 0)
        for part in range(1, p.heads + 1):
            for k in range(last):
                waiting.append((part, k))

    waiting = []

    def tick():
        if waiting:
            part, k = waiting.pop(0)
            w_pass(part, k)
            if k == last - 1 and part < p.heads:
                w_begin(part + 1)

    def drain(part):
        while waiting and waiting[0][0] <= part:
            tick()
        w_finish(part)

    def ready(head):
        drain(head)
        project_rows(p, r, head)

    def out_ready():
        drain(p.heads)

    def after():
        saves.extend(moves(r, [(r.all_w, r.all_w_out), (r.disp, r.disp_out), (r.comb, r.comb_out)]))
        experts_pass()

    total = attention_forward(p, r, r.a, 0, state, before, ready, tick, out_ready, after)
    middle = state + total.T
    r.middle[...] = middle
    m = (norm_parts(middle)[1] * r.gain_two[...].astype(F32)).astype(BF)
    r.outgoing[...] = mm(r.disp[0], m).astype(BF)
    there = slot_sends(p, r.outgoing, r.arrived, (r.go_s, r.go_r), slot_peer)
    saves.extend(moves(r, [(getattr(r.a, k), getattr(r, k + "_out")) for k in SAVED]))
    for copy in tables:
        copy.wait_recv()
    slot_pairs(p, r)
    for copy in beside:
        copy.wait_recv()
    arrive(local)
    saves.extend(moves(r, [(r.all_in, r.all_in_out), (r.all_back, r.all_back_out), (r.pair, r.pair_end)]))
    back = {}
    for at, sources in slot_groups(p):
        receive(there, sources)
        rows = r.arrived[at, :]
        out = expert_output(p, r, rows, at, False)
        r.produced[at, :] = out.astype(BF)
        r.ret_out[at, :] = (out * slot_gates(p, r, rows, r.pair[0, at, :].astype(F32))).astype(BF)
        for s in sources:
            if s:
                back[s] = slot_send(p, r.ret_out, r.ret_in, (r.ret_s, r.ret_r), s, slot_source(p, s))
    r.ret_in[0 : p.cap, :] = r.ret_out[0 : p.cap, :]
    receive(back, range(p.experts))
    r.first[...] = r.middle[...] + mm(r.comb[0], r.ret_in[...])
    sent(there)
    sent(back)
    sent(tables)
    sent(beside)
    w_end()
    sent(over)
    picks.end()
    arrive(saves)


def turn_kernel(p, r):
    peers = pack_peers(p) + slot_peers(p)
    greet(peers)
    early = moves(
        r, [(r.disp_in.at[1], r.disp), (r.all_w_in, r.all_w), (r.comb_in.at[1], r.comb), (r.pair_in.at[1], r.pair)]
    )
    fill_router(p, r)
    weights = moves(r, [(r.all_in_in, r.all_in), (r.all_back_in, r.all_back)])
    first = r.first[...]
    stop = 1.0 / (1.0 + jnp.exp(-jnp.sum(first * r.halt[...].astype(F32), axis=-1, keepdims=True)))
    cot = r.cot[...].astype(F32)
    segment_columns(p, r.segments, r.seg_cols)
    answered(peers)
    there_u, saves = {}, []

    def before(gather):
        arrive(early)
        r.u_out[...] = mm(r.disp[...], ((1.0 - stop) * cot).astype(BF)).astype(BF)
        there_u.update(slot_sends(p, r.u_out, r.u_in, (r.u_s, r.u_r), slot_peer))
        for head in range(p.heads):
            project_rows(p, r, head)

    def nothing(*_):
        pass

    total = attention_forward(p, r, r.a, 1, first, before, nothing, nothing, nothing, nothing)
    middle = first + total.T
    r.middle[...] = middle
    m = (norm_parts(middle)[1] * r.gain_two[...].astype(F32)).astype(BF)
    r.outgoing[...] = mm(r.disp[...], m).astype(BF)
    there = slot_sends(p, r.outgoing, r.arrived, (r.go_s, r.go_r), slot_peer)
    transposed(r.wo, r.all_w, 0, p.qkv, p.all_cols, LANES)
    attention_rows(p, r, r.a, False)
    arrive(weights)
    sent(there_u)
    ret_out = r.u_out
    back, back_out = {}, {}
    for at, sources in slot_groups(p):
        receive(there_u, sources)
        receive(there, sources)
        rows = r.arrived[at, :]
        pair = r.pair[at, :].astype(F32)
        out = expert_output(p, r, rows, at, True)
        ret_out[at, :] = (out * slot_gates(p, r, rows, pair)).astype(BF)
        expert_input_grad(p, r, at, r.u_in[at, :].astype(F32), rows, out, pair, r.gret_out)
        for s in sources:
            if s:
                back[s] = slot_send(p, r.gret_out, r.gret_in, (r.gret_s, r.gret_r), s, slot_source(p, s))
    r.gret_in[0 : p.cap, :] = r.gret_out[0 : p.cap, :]
    r.ret_in[0 : p.cap, :] = ret_out[0 : p.cap, :]
    r.grad_router[...] = expert_weight_grads(p, r, r.arrived, False)
    saves.extend(moves(r, [(r.grad_in, r.grad_in_out), (r.grad_back, r.grad_back_out)]))
    attention_probs(p, r, r.a)
    receive(back, range(p.experts))
    step_back, gain_two = norm_back(r.middle[...], r.gain_two[...].astype(F32), mm(r.comb[...], r.gret_in[...]))
    r.grad_gain_two[...] = gain_two
    grad_middle = (1.0 - stop) * cot + step_back

    def before_back():
        for s in range(1, p.experts):
            back_out[s] = slot_send(p, ret_out, r.ret_in, (r.ret_s, r.ret_r), s, slot_source(p, s))

    def head_done(head):
        if head == p.heads - 1:
            for part in p.parts:
                attention_weight_grads(p, r, r.a, part.start, part.stop, False)

    grad, gain_one, router = attention_backward(
        p, r, r.a, 1, first, grad_middle, before_back, lambda: None, head_done
    )
    saves.extend(moves(r, [(r.grad_w, r.grad_w_out)]))
    r.grad_gain_one[...] = gain_one
    r.grad_mixer[...] = router
    receive(back_out, range(p.experts))
    second = r.middle[...] + mm(r.comb[...], r.ret_in[...])
    r.result[...] = (stop * first + (1.0 - stop) * second).astype(BF)
    grad_stop = jnp.sum(cot * (first - second), axis=-1, keepdims=True)
    coeff = grad_stop * stop * (1.0 - stop)
    r.grad_halt[...] = jnp.sum(coeff * first, axis=0, keepdims=True)
    r.grad_first[...] = stop * cot + coeff * r.halt[...].astype(F32) + grad
    for copies in (there, back, back_out):
        sent(copies)
    arrive(saves)


def backward_kernel(p, r):
    b, d = place()
    z, x = d // p.lo, lax.rem(d, p.lo)
    y, c = b // 2, lax.rem(b, 2)
    e, g = b // p.group, lax.rem(b, p.group)
    rows = r.out_w.shape[0]
    in_rows, back_rows = r.out_in.shape[1], r.out_back.shape[1]
    peers = pack_peers(p) + slot_peers(p) + dp_peers(p) + expert_peers(p)
    greet(peers)
    early = moves(
        r,
        [
            (r.disp_in.at[0], r.disp),
            (r.pair_in.at[0], r.pair),
            (r.arrived_in, r.arrived),
            (r.all_in_in, r.all_in),
            (r.all_back_in, r.all_back),
            (r.produced_in, r.produced),
        ],
    )
    later = moves(
        r, [(r.grad_in_in, r.grad_in), (r.grad_back_in, r.grad_back), (r.comb_in.at[0], r.comb), (r.all_w_in, r.all_w)]
    )
    later += moves(r, [(r.grad_w_in, r.grad_w)])
    later += moves(r, [(getattr(r, k + "_in"), getattr(r.a, k)) for k in SAVED])
    fill_router(p, r)
    grad_first = r.grad_first[...]
    early[0].wait()
    r.u_out[...] = mm(r.disp[...], grad_first.astype(BF)).astype(BF)
    answered(peers)
    there = slot_sends(p, r.u_out, r.u_in, (r.u_s, r.u_r), slot_peer)
    arrive(early[1:])
    for at, _ in slot_groups(p):
        expert_keep(p, r, r.arrived[at, :], at)
    segment_columns(p, r.segments, r.seg_cols)
    arrive(later)
    attention_rows(p, r, r.a, True)
    transposed(r.wo, r.all_w, 0, p.qkv, p.all_cols, LANES)
    back = {}
    for at, sources in slot_groups(p):
        receive(there, sources)
        pair = r.pair[at, :].astype(F32)
        out = r.produced[at, :].astype(F32)
        expert_input_grad(p, r, at, r.u_in[at, :].astype(F32), r.arrived[at, :], out, pair, r.produced)
        for s in sources:
            if s:
                back[s] = slot_send(p, r.produced, r.gret_in, (r.gret_s, r.gret_r), s, slot_source(p, s))
    r.gret_in[0 : p.cap, :] = r.produced[0 : p.cap, :]
    r.grad_router[...] = expert_weight_grads(p, r, r.arrived, True)

    def row_block(ref, index, size, lanes=slice(None)):
        return ref.at[pl.ds(aligned(index * size, size), size), lanes]

    near = {}
    for k in range(p.local):
        to = turn(e, k + 1, p.local)
        for t in range(1, p.group):
            member = turn(g, t, p.group)
            slot = k * (p.group - 1) + t - 1
            peer = (e * p.group + member, d)
            owner = to * p.group + member
            near[k, t, 0] = send(
                row_block(r.grad_in, owner, in_rows), r.in_near.at[slot], (r.near_s, r.near_r), 2 * slot, peer
            )
            near[k, t, 1] = send(
                row_block(r.grad_back, owner, back_rows), r.back_near.at[slot], (r.near_s, r.near_r), 2 * slot + 1, peer
            )
    attention_probs(p, r, r.a)
    receive(back, range(p.experts))
    step_back, gain_two = norm_back(r.middle[...], r.gain_two[...].astype(F32), mm(r.comb[...], r.gret_in[...]))
    grad_middle = grad_first + step_back
    wide, lo_copies, hi_copies = {}, {}, {}

    def experts_wide():
        for k in range(p.local):
            to = turn(e, k + 1, p.local)
            total_in = row_block(r.grad_in, to * p.group + g, in_rows)[...].astype(F32)
            total_back = row_block(r.grad_back, to * p.group + g, back_rows)[...].astype(F32)
            for t in range(1, p.group):
                slot = k * (p.group - 1) + t - 1
                near[k, t, 0].wait_recv()
                near[k, t, 1].wait_recv()
                total_in = total_in + r.in_near[slot].astype(F32)
                total_back = total_back + r.back_near[slot].astype(F32)
            if k < p.local - 1:
                r.in_far_out[k] = total_in.astype(BF)
                r.back_far_out[k] = total_back.astype(BF)
                peer = (to * p.group + g, d)
                wide[k, 0] = send(r.in_far_out.at[k], r.in_far.at[k], (r.wide_s, r.wide_r), 2 * k, peer)
                wide[k, 1] = send(r.back_far_out.at[k], r.back_far.at[k], (r.wide_s, r.wide_r), 2 * k + 1, peer)
            else:
                r.out_in[e] = total_in.astype(BF)
                r.out_back[e] = total_back.astype(BF)

    parts = p.parts

    def sum_begin(part):
        for k in range(p.hi):
            to = turn(z, k + 1, p.hi)
            for t in range(1, p.lo):
                slot = k * (p.lo - 1) + t - 1
                xx = turn(x, t, p.lo)
                lo_copies[part, k, t] = send(
                    row_block(r.grad_w, to * p.lo + xx, rows, parts[part]),
                    r.w_lo.at[slot, :, parts[part]],
                    (r.lo_s, r.lo_r),
                    part * p.hi * (p.lo - 1) + slot,
                    (b, z * p.lo + xx),
                )

    def sum_pass(part):
        lanes = parts[part]
        for k in range(p.hi):
            to = turn(z, k + 1, p.hi)
            total = row_block(r.grad_w, to * p.lo + x, rows, lanes)[...].astype(F32)
            for t in range(1, p.lo):
                lo_copies[part, k, t].wait_recv()
                total = total + r.w_lo[k * (p.lo - 1) + t - 1, :, lanes].astype(F32)
            if k < p.hi - 1:
                r.w_hi_out[k, :, lanes] = total.astype(BF)
                hi_copies[part, k] = send(
                    r.w_hi_out.at[k, :, lanes],
                    r.w_hi.at[k, :, lanes],
                    (r.hi_s, r.hi_r),
                    part * (p.hi - 1) + k,
                    (b, to * p.lo + x),
                )
            else:
                r.out_w[:, lanes] = total

    def sum_finish(part):
        lanes = parts[part]
        total = r.out_w[:, lanes]
        for k in range(p.hi - 1):
            hi_copies[part, k].wait_recv()
            total = total + r.w_hi[k, :, lanes].astype(F32)
        r.out_w[:, lanes] = total

    def middle():
        experts_wide()
        attention_weight_grads(p, r, r.a, p.qkv, p.all_cols, True)
        sum_begin(p.heads)

    def head_done(head):
        attention_weight_grads(p, r, r.a, parts[head].start, parts[head].stop, True)
        sum_begin(head)
        sum_pass(p.heads if head == 0 else head - 1)

    grad, gain_one, router = attention_backward(
        p, r, r.a, 0, r.x[...].astype(F32), grad_middle, lambda: None, middle, head_done
    )
    small = r.out_small
    small[...] = jnp.zeros_like(small)
    small[0:1, :] = r.gain_one_before[...] + gain_one
    small[1:2, :] = r.gain_two_before[...] + gain_two
    small[2:3, :] = r.halt_before[...]
    small[8 : 8 + p.mixers, :] = r.mixer_before[...] + router
    small[8 + p.mixers :, :] = r.router_before[...] + r.grad_router[...]
    tiny = []
    axes = (
        (2, c, lambda t: (2 * y + turn(c, t, 2), d)),
        (p.chips, y, lambda t: (2 * turn(y, t, p.chips) + c, d)),
        (p.lo, x, lambda t: (b, z * p.lo + turn(x, t, p.lo))),
        (p.hi, z, lambda t: (b, turn(z, t, p.hi) * p.lo + x)),
    )

    def tiny_begin(axis):
        size, index, peer = axes[axis]
        base = sum(entry[0] for entry in axes[:axis])
        r.all_small[base + index] = small[...]
        at = r.all_small.at[base + index]
        for t in range(1, size):
            tiny.append(send(at, at, (r.tiny_s, r.tiny_r), base + t - 1, peer(t)))

    def tiny_finish(axis):
        size = axes[axis][0]
        base = sum(entry[0] for entry in axes[:axis])
        for copy in tiny[len(tiny) - (size - 1) :]:
            copy.wait_recv()
        total = r.all_small[base]
        for k in range(1, size):
            total = total + r.all_small[base + k]
        small[...] = total

    tiny_begin(0)
    r.input_grad[...] = grad.astype(BF)
    tiny_finish(0)
    tiny_begin(1)
    sum_pass(p.heads - 1)
    tiny_finish(1)
    tiny_begin(2)
    for k in range(p.local - 1):
        source = turn(e, -(k + 1), p.local)
        wide[k, 0].wait_recv()
        wide[k, 1].wait_recv()
        r.out_in[source] = r.in_far[k]
        r.out_back[source] = r.back_far[k]
    tiny_finish(2)
    tiny_begin(3)
    sum_finish(p.heads)
    for part in range(p.heads - 1):
        sum_finish(part)
    tiny_finish(3)
    sum_finish(p.heads - 1)
    for copies in (there, back, near, wide, lo_copies, hi_copies, tiny):
        sent(copies)


def output_kernel(p, r):
    cols = p.cols
    r.result_out[...] = r.result[...]
    r.input_grad_out[...] = r.input_grad[...]
    r.in_out[...] = r.out_in[...].astype(F32)
    r.back_out[...] = r.out_back[...].astype(F32)
    for e in range(p.mixers):
        heads = [h * p.head_cols + e * HD for h in range(p.heads)]
        r.query_out[e] = jnp.concatenate([r.out_w[:, at : at + HD] for at in heads], axis=1)
        start = p.qkv + e * cols
        r.out_out[e] = r.out_w[:, start : start + cols]
    heads = [h * p.head_cols + p.mixers * HD for h in range(p.heads)]
    r.key_out[...] = jnp.concatenate([r.out_w[:, at : at + HD] for at in heads], axis=1)
    r.value_out[...] = jnp.concatenate([r.out_w[:, at + HD : at + 2 * HD] for at in heads], axis=1)
    r.gain_one_out[...] = r.small[0:1, :]
    r.gain_two_out[...] = r.small[1:2, :]
    r.halt_out[...] = r.small[2:3, :]
    r.mixer_out[...] = r.small[8 : 8 + p.mixers, :]
    r.router_out[...] = r.small[8 + p.mixers :, :]


SAVED = ("nt", "qs", "kt", "vt", "lse", "att", "mix", "gates")


def dma(name, size):
    sem = pltpu.SemaphoreType.DMA((max(1, size),))
    return {name + "_s": sem, name + "_r": sem}


def pack_sems(p, name):
    sizes = (p.chips - 1, p.chips - 1, p.chips, p.chips)
    return {f"{name}_{k}": pltpu.SemaphoreType.DMA((max(1, size),)) for k, size in enumerate(sizes)}


def sum_scratch(p):
    far = max(1, p.chips - 1)
    return {
        "part": pltpu.VMEM((p.chips, p.width, p.seq), BF),
        "near_in": pltpu.VMEM((p.chips, p.width, p.seq), BF),
        "far_out": pltpu.VMEM((far, p.width, p.seq), BF),
        "far_in": pltpu.VMEM((far, p.width, p.seq), BF),
    }


def saved_shapes(p):
    return {
        "nt": ((p.blk, p.width, p.seq), BF),
        "qs": ((p.heads, p.blocks, HD, p.top * QROWS), BF),
        "kt": ((p.heads, HD, p.length + MAXLEN), BF),
        "vt": ((p.heads, HD, p.length + MAXLEN), BF),
        "lse": ((p.blocks, 8, p.top * QROWS), F32),
        "att": ((p.heads, p.blocks, HD, p.top * QROWS), BF),
        "mix": ((p.mixers * p.cols, p.length), BF),
        "gates": ((p.blk, 8, p.seq), F32),
    }


def launch(body, name, number, ins, outs, scratch):
    def spec(vmem):
        return pl.BlockSpec(memory_space=pltpu.VMEM if vmem else pl.ANY)

    names = list(ins) + list(outs) + list(scratch)

    def kernel(*refs):
        r = SimpleNamespace(**dict(zip(names, refs, strict=True)))
        r.moved = 0
        r.a = SimpleNamespace(**{k[2:]: v for k, v in vars(r).items() if k.startswith("a_")})
        for key in ("gather", "sum", "back_gather", "back_sum", "picks"):
            sems = [getattr(r, f"{key}_{k}") for k in range(4) if hasattr(r, f"{key}_{k}")]
            setattr(r.a, key + "_sems", sems)
            setattr(r, key + "_sems", sems)
        body(r)

    results = pl.pallas_call(
        kernel,
        out_shape=tuple(jax.ShapeDtypeStruct(shape, dtype) for shape, dtype, _ in outs.values()),
        in_specs=[spec(vmem) for _, vmem in ins.values()],
        out_specs=tuple(spec(vmem) for _, _, vmem in outs.values()),
        scratch_shapes=list(scratch.values()),
        compiler_params=pltpu.CompilerParams(
            collective_id=number, has_side_effects=number is not None, vmem_limit_bytes=VMEM_BYTES
        ),
        name=name,
    )(*[array for array, _ in ins.values()])
    return SimpleNamespace(**dict(zip(outs, results, strict=True)))


def on_device(
    inputs,
    segments,
    attention_routes,
    expert_routes,
    gain_mixer,
    gain_expert,
    weight_query,
    weight_key,
    weight_value,
    weight_out,
    router_mixer,
    router_expert,
    weight_in,
    weight_back,
    halt_weight,
    cotangent,
):
    blk, dp = lax.axis_size("blk"), lax.axis_size("dp")
    seq, width = inputs.shape[1:]
    experts, local = router_expert.shape[1], weight_in.shape[0]
    slots_of = max(2, 3 * seq // experts)
    hi = 4
    p = Plan(
        blk=blk,
        dp=dp,
        lo=dp // hi,
        hi=hi,
        seq=seq,
        width=width,
        heads=HEADS // blk,
        mixers=weight_query.shape[0],
        top=attention_routes.shape[-1],
        experts=experts,
        local=local,
        group=blk // local,
        cap=-(-slots_of // 16) * 16,
        ff=weight_in.shape[2],
    )
    cols, length, top = p.cols, p.length, p.top
    share, in_rows, back_rows = weight_key.shape[0], weight_in.shape[1], weight_back.shape[1]

    gain_one = gain_mixer.reshape(1, width)
    gain_two = gain_expert.reshape(1, width)
    halt = halt_weight.reshape(1, width)
    router_row, router = router_mixer.T, router_expert.T

    slots_bf = pltpu.VMEM((p.slots, width), BF)
    saved = saved_shapes(p)
    attention_scratch = {
        "seg_cols": pltpu.VMEM((length + MAXLEN, 8), F32),
        "k_rows": pltpu.VMEM((p.heads, length + MAXLEN, HD), BF),
        "all_w": pltpu.VMEM((width, p.all_cols), BF),
        **{"a_" + k: pltpu.VMEM(*v) for k, v in saved.items()},
    }
    forward_scratch = {
        "w_t": pltpu.VMEM((p.qkv, width), BF),
        **pack_sems(p, "gather"),
        **pack_sems(p, "sum"),
        **sum_scratch(p),
    }
    backward_scratch = {
        "gt": pltpu.VMEM((blk, width, seq), BF),
        "v_rows": pltpu.VMEM((p.heads, length + MAXLEN, HD), BF),
        "means": pltpu.VMEM((p.blocks, 8, top * QROWS), F32),
        "dlog": pltpu.VMEM((blk, p.mixers, seq), F32),
        "dkt": pltpu.VMEM((p.heads, HD, length + MAXLEN), F32),
        "dvt": pltpu.VMEM((p.heads, HD, length + MAXLEN), F32),
        "dall": pltpu.VMEM((p.qkv, length), BF),
        "grad_w": pltpu.VMEM((width, p.all_cols), BF),
        **pack_sems(p, "back_gather"),
        **pack_sems(p, "back_sum"),
        **sum_scratch(p),
    }
    expert_scratch = {
        "router": pltpu.VMEM((LANES, width), BF),
        "all_in": pltpu.VMEM((width, p.ff), BF),
        "all_back": pltpu.VMEM((p.ff, width), BF),
    }
    expert_back_scratch = {
        "keep": pltpu.VMEM((2, p.slots, p.ff), BF),
        "coeff": pltpu.VMEM((p.slots, LANES), BF),
        "arrived_t": pltpu.VMEM((width, p.slots), BF),
        "u_out": slots_bf,
        "u_in": slots_bf,
        "gret_in": slots_bf,
        "grad_in": pltpu.VMEM((width, p.ff), BF),
        "grad_back": pltpu.VMEM((p.ff, width), BF),
        **dma("u", p.experts),
        **dma("gret", p.experts),
    }

    one = launch(
        functools.partial(forward_kernel, p),
        "forward",
        0,
        {
            "x": (inputs[0], True),
            "segments": (segments, True),
            "attention_routes": (jnp.swapaxes(attention_routes[:, 0], 1, 2), True),
            "expert_routes": (jnp.swapaxes(expert_routes[:, 0], 1, 2), True),
            "gain_one": (gain_one, True),
            "gain_two": (gain_two, True),
            "router_row": (router_row, True),
            "router_in": (router, True),
            "weight_query": (weight_query, True),
            "weight_key": (weight_key, True),
            "weight_value": (weight_value, True),
            "weight_out": (jnp.swapaxes(weight_out, 1, 2), True),
            "weight_in": (weight_in, False),
            "weight_back": (weight_back, False),
        },
        {
            "first": ((seq, width), F32, True),
            "middle": ((seq, width), F32, True),
            "arrived": ((p.slots, width), BF, True),
            "produced": ((p.slots, width), BF, True),
            "all_picks": ((blk, 16, seq), jnp.int32, True),
            "disp_out": ((2, p.slots, seq), BF, False),
            "comb_out": ((2, seq, p.slots), BF, False),
            "pair_end": ((2, p.slots, LANES), BF, False),
            "all_w_out": ((width, p.all_cols), BF, False),
            "all_in_out": ((width, p.ff), BF, False),
            "all_back_out": ((p.ff, width), BF, False),
            **{k + "_out": (*v, False) for k, v in saved.items()},
        },
        {
            **attention_scratch,
            **forward_scratch,
            **expert_scratch,
            "disp": pltpu.VMEM((2, p.slots, seq), BF),
            "comb": pltpu.VMEM((2, seq, p.slots), BF),
            "pair": pltpu.VMEM((2, p.slots, LANES), BF),
            "pair_out": pltpu.VMEM((experts, 8, LANES), F32),
            "pair_in": pltpu.VMEM((experts, 8, LANES), F32),
            "routes": pltpu.VMEM((16, seq), jnp.int32),
            "outgoing": slots_bf,
            "ret_out": slots_bf,
            "ret_in": slots_bf,
            **pack_sems(p, "picks"),
            **dma("hi", 2 * (p.heads + 1) * (p.hi - 1)),
            **dma("lo", (p.heads + 1) * p.hi * (p.lo - 1)),
            **dma("wide", 2 * (p.local - 1)),
            **dma("near", 2 * p.local * (p.group - 1)),
            **dma("pair", p.experts),
            **dma("go", p.experts),
            **dma("ret", p.experts),
            "moves": pltpu.SemaphoreType.DMA((16,)),
        },
    )
    two = launch(
        functools.partial(turn_kernel, p),
        "turn",
        1,
        {
            "first": (one.first, True),
            "cot": (cotangent[0], True),
            "halt": (halt, True),
            "segments": (segments, True),
            "all_picks": (one.all_picks, True),
            "gain_one": (gain_one, True),
            "gain_two": (gain_two, True),
            "router_row": (router_row, True),
            "router_in": (router, True),
            "disp_in": (one.disp_out, False),
            "comb_in": (one.comb_out, False),
            "pair_in": (one.pair_end, False),
            "all_w_in": (one.all_w_out, False),
            "all_in_in": (one.all_in_out, False),
            "all_back_in": (one.all_back_out, False),
        },
        {
            "result": ((seq, width), BF, True),
            "grad_first": ((seq, width), F32, True),
            "grad_halt": ((1, width), F32, True),
            "grad_gain_one": ((1, width), F32, True),
            "grad_gain_two": ((1, width), F32, True),
            "grad_mixer": ((p.mixers, width), F32, True),
            "grad_router": ((experts, width), F32, True),
            "grad_in_out": ((width, p.ff), BF, False),
            "grad_back_out": ((p.ff, width), BF, False),
            "grad_w_out": ((width, p.all_cols), BF, False),
        },
        {
            **attention_scratch,
            **forward_scratch,
            **backward_scratch,
            **expert_scratch,
            **expert_back_scratch,
            "wo": pltpu.VMEM((p.mixers * cols, width), BF),
            "disp": pltpu.VMEM((p.slots, seq), BF),
            "comb": pltpu.VMEM((seq, p.slots), BF),
            "pair": pltpu.VMEM((p.slots, LANES), BF),
            "middle": pltpu.VMEM((seq, width), F32),
            "outgoing": slots_bf,
            "arrived": slots_bf,
            "gret_out": slots_bf,
            "ret_in": slots_bf,
            **dma("go", p.experts),
            **dma("ret", p.experts),
            "moves": pltpu.SemaphoreType.DMA((16,)),
        },
    )
    near, far = p.local * (p.group - 1), max(1, p.local - 1)
    small_rows = 8 + p.mixers + experts
    three = launch(
        functools.partial(backward_kernel, p),
        "backward",
        2,
        {
            "x": (inputs[0], True),
            "grad_first": (two.grad_first, True),
            "middle": (one.middle, True),
            "segments": (segments, True),
            "all_picks": (one.all_picks, True),
            "gain_one": (gain_one, True),
            "gain_two": (gain_two, True),
            "router_row": (router_row, True),
            "router_in": (router, True),
            "halt_before": (two.grad_halt, True),
            "gain_one_before": (two.grad_gain_one, True),
            "gain_two_before": (two.grad_gain_two, True),
            "mixer_before": (two.grad_mixer, True),
            "router_before": (two.grad_router, True),
            "disp_in": (one.disp_out, False),
            "comb_in": (one.comb_out, False),
            "pair_in": (one.pair_end, False),
            "arrived_in": (one.arrived, False),
            "produced_in": (one.produced, False),
            "all_w_in": (one.all_w_out, False),
            "all_in_in": (one.all_in_out, False),
            "all_back_in": (one.all_back_out, False),
            "grad_in_in": (two.grad_in_out, False),
            "grad_back_in": (two.grad_back_out, False),
            "grad_w_in": (two.grad_w_out, False),
            **{k + "_in": (getattr(one, k + "_out"), False) for k in SAVED},
        },
        {
            "input_grad": ((seq, width), BF, True),
            "out_w": ((share, p.all_cols), F32, True),
            "out_in": ((local, in_rows, p.ff), BF, True),
            "out_back": ((local, back_rows, width), BF, True),
            "out_small": ((small_rows, width), F32, True),
        },
        {
            **attention_scratch,
            **backward_scratch,
            **expert_scratch,
            **expert_back_scratch,
            "wo": pltpu.VMEM((p.mixers * cols, width), BF),
            "disp": pltpu.VMEM((p.slots, seq), BF),
            "comb": pltpu.VMEM((seq, p.slots), BF),
            "pair": pltpu.VMEM((p.slots, LANES), BF),
            "arrived": slots_bf,
            "produced": slots_bf,
            "in_near": pltpu.VMEM((near, in_rows, p.ff), BF),
            "back_near": pltpu.VMEM((near, back_rows, width), BF),
            "in_far_out": pltpu.VMEM((far, in_rows, p.ff), BF),
            "in_far": pltpu.VMEM((far, in_rows, p.ff), BF),
            "back_far_out": pltpu.VMEM((far, back_rows, width), BF),
            "back_far": pltpu.VMEM((far, back_rows, width), BF),
            "w_lo": pltpu.VMEM((hi * (p.lo - 1), share, p.all_cols), BF),
            "w_hi_out": pltpu.VMEM((hi - 1, share, p.all_cols), BF),
            "w_hi": pltpu.VMEM((hi - 1, share, p.all_cols), BF),
            "grad_router": pltpu.VMEM((experts, width), F32),
            "all_small": pltpu.VMEM((2 + p.chips + p.lo + hi, small_rows, width), F32),
            **dma("near", 2 * near),
            **dma("wide", 2 * (local - 1)),
            **dma("lo", (p.heads + 1) * hi * (p.lo - 1)),
            **dma("hi", (p.heads + 1) * (hi - 1)),
            **dma("tiny", 2 + p.chips + p.lo + hi),
            "moves": pltpu.SemaphoreType.DMA((24,)),
        },
    )
    four = launch(
        functools.partial(output_kernel, p),
        "outputs",
        None,
        {
            "result": (two.result, True),
            "input_grad": (three.input_grad, True),
            "out_w": (three.out_w, True),
            "out_in": (three.out_in, True),
            "out_back": (three.out_back, True),
            "small": (three.out_small, True),
        },
        {
            "result_out": ((seq, width), BF, True),
            "input_grad_out": ((seq, width), BF, True),
            "query_out": (weight_query.shape, F32, True),
            "key_out": (weight_key.shape, F32, True),
            "value_out": (weight_value.shape, F32, True),
            "out_out": ((p.mixers, share, cols), F32, True),
            "in_out": (weight_in.shape, F32, True),
            "back_out": (weight_back.shape, F32, True),
            "gain_one_out": ((1, width), F32, True),
            "gain_two_out": ((1, width), F32, True),
            "halt_out": ((1, width), F32, True),
            "mixer_out": ((p.mixers, width), F32, True),
            "router_out": ((experts, width), F32, True),
        },
        {},
    )
    return (
        four.result_out[None],
        four.input_grad_out[None],
        four.gain_one_out.reshape(width),
        four.gain_two_out.reshape(width),
        four.query_out,
        four.key_out,
        four.value_out,
        jnp.swapaxes(four.out_out, 1, 2),
        four.mixer_out.T,
        four.router_out.T,
        four.in_out,
        four.back_out,
        four.halt_out.reshape(width),
    )


def solution(mesh):
    return jax.shard_map(
        on_device,
        mesh=mesh,
        in_specs=(
            P("dp", "blk", None),
            P("dp", None),
            P(None, "dp", "blk", None),
            P(None, "dp", "blk", None),
            P(),
            P(),
            P(None, "dp", "blk"),
            P("dp", "blk"),
            P("dp", "blk"),
            P(None, "blk", "dp"),
            P(),
            P(),
            P("dp", "blk", None),
            P("dp", "blk", None),
            P(),
            P("dp", "blk", None),
        ),
        out_specs=(
            P("dp", "blk", None),
            P("dp", "blk", None),
            P(),
            P(),
            P(None, "dp", "blk"),
            P("dp", "blk"),
            P("dp", "blk"),
            P(None, "blk", "dp"),
            P(),
            P(),
            P("dp", "blk", None),
            P("dp", "blk", None),
            P(),
        ),
        check_vma=False,
    )
```

profile of v0, /device:TPU:0, one launch (start us, length us, event | category | flops | bytes accessed | tf_op | source)
XLA Modules:
  0.0 309.7 jit_solution(4401742955512114504)
XLA Ops:
  0.6 0.0 copy-start
  0.7 1.3 reshape.44.refs_4_.refs_5_
  1.9 1.3 reshape.45.refs_5_.refs_6_
  3.2 94.0 %forward.1 = (f32[256,512]{1,0:T(8,128)}, f32[256,512]{1,0:T(8,128)}, bf16[768,512]{1,0:T(8,128)(2,1)}, bf16[768,512]{1,0:T(8,128)(2,1)}, s32[4,16,256]{2,1,0:T(...) custom-call(bf16[256,512]{1,0:T(8,128)(2,1)} %bitcast.19, ...), custom_call_target="tpu_custom_call" | custom-call | tf_op jit(solution)/shard_map/forward/pallas_call | solution.py:1304
  97.2 0.0 copy-done
  97.2 0.6 reshape.46.refs_2_
  97.8 104.5 %turn.1 = (bf16[256,512]{1,0:T(8,128)(2,1)}, f32[256,512]{1,0:T(8,128)}, f32[1,512]{1,0:T(1,128)}, f32[1,512]{1,0:T(1,128)}, f32[1,512]{1,0:T(1,128)}, /*index=5...) custom-call(f32[256,512]{1,0:T(8,128)} %get-tuple-element.60.refs_0_, ...), custom_call_target="tpu_custom_call" | custom-call | tf_op jit(solution)/shard_map/turn/pallas_call | solution.py:1304
  202.3 102.7 %backward.1 = (bf16[256,512]{1,0:T(8,128)(2,1)}, f32[64,2304]{1,0:T(8,128)}, bf16[2,128,2048]{2,1,0:T(8,128)(2,1)}, bf16[2,512,512]{2,1,0:T(8,128)(2,1)}, f32[32,512]{1,0:T(8,128)}) custom-call(bf16[256,512]{1,0:T(8,128)(2,1)} %bitcast.20, f32[256,512]{1,0:T(8,128)} %get-tuple-element.69.refs_1_, f32[256,512]{1,0:T(8,128)} %get-tuple-element.70.refs_2_, ...), custom_call_target="tpu_custom_call" | custom-call | tf_op jit(solution)/shard_map/backward/pallas_call | solution.py:1304
  305.0 4.4 %outputs.1 = (bf16[256,512]{1,0:T(8,128)(2,1)}, bf16[256,512]{1,0:T(8,128)(2,1)}, f32[8,64,128]{2,1,0:T(8,128)}, f32[64,128]{1,0:T(8,128)}, f32[64,128]{1,0:T(8,...) custom-call(bf16[256,512]{1,0:T(8,128)(2,1)} %get-tuple-element.68.r, ...), custom_call_target="tpu_custom_call" | custom-call | tf_op jit(solution)/shard_map/outputs/pallas_call | solution.py:1304
Async XLA Ops:
  0.6 96.6 %copy-start = (bf16[512]{0:T(512)(128)(2,1)S(1)}, bf16[512]{0:T(512)(128)(2,1)}, u32[]{:S(2)}) copy-start(bf16[512]{0:T(512)(128)(2,1)} %param.30) | copy-start | bytes 3076
where the time goes:
time: 315 us; the launch traced here: 310 us
  Pallas kernels  306 us (97%)
    pallas_call x4, Pallas kernels, launch(): pl.pallas_call(kernel, out_shape=tuple((jax.ShapeDtypeStruct(shape, dtype...  306 us

commit v1 on v0

--- a/solution.py
+++ b/solution.py
@@ -404,16 +404,20 @@
             a.mix[rows, pl.ds(start, QROWS)] = spread_rows(p, table, values, e).astype(BF)
 
 
+def by_head(p):
+    return [[head] for head in range(p.heads)]
+
+
 def each_block(work, first, count):
     @pl.loop(0, count)
     def _(k):
         work(first + k)
 
 
-def attention_forward(p, r, a, step, state, before, ready, tick, out_ready, after):
+def attention_forward(p, r, a, step, state, passes, before, ready, tick, out_ready, after):
     b, _ = place()
     y, c = b // 2, lax.rem(b, 2)
-    a.nt[b] = (norm_parts(state)[1] * r.gain_one[...].astype(F32)).T.astype(BF)
+    a.nt[b] = (norm_parts(state)[1] * r.vectors[0:1, :].astype(F32)).T.astype(BF)
     gather = PackGather(p, a.nt, a.gather_sems)
     gather.begin()
     r.k_rows[:, 0:MAXLEN, :] = jnp.zeros((p.heads, MAXLEN, HD), BF)
@@ -425,39 +429,44 @@
     def branch(bb):
         return mm(r.all_w[:, p.qkv :], a.mix[:, pl.ds(aligned(bb * p.seq, p.seq), p.seq)])
 
-    for head in range(p.heads):
-        if head == 0:
-            project(p, r, a, step, b, head)
+    def attends(bb, heads):
+        for head in heads:
+            attend(p, r, a, step, bb, head)
+        tick()
+
+    def projects(bb, heads):
+        for head in heads:
+            project(p, r, a, step, bb, head)
+
+    for heads in passes:
+        final = heads[-1] == p.heads - 1
+        if heads[0] == 0:
+            projects(b, heads)
             gather.finish_near()
-            project(p, r, a, step, 2 * y + 1 - c, head)
+            projects(2 * y + 1 - c, heads)
             tick()
-            attend(p, r, a, step, 2 * y + 1, head)
+            attends(2 * y + 1, heads)
             gather.finish_far()
-            tick()
             for s in range(1, p.chips):
-                each_block(lambda bb: project(p, r, a, step, bb, 0), 2 * turn(y, s, p.chips), 2)
+                each_block(lambda bb: projects(bb, heads), 2 * turn(y, s, p.chips), 2)
             tick()
         else:
-            ready(head)
-            each_block(lambda bb: project(p, r, a, step, bb, head), 0, p.blk)
-            attend(p, r, a, step, 2 * y + 1, head)
-            tick()
+            ready(heads[0])
+            each_block(lambda bb: projects(bb, heads), 0, p.blk)
+            attends(2 * y + 1, heads)
         for s in range(1, p.chips):
             yy = turn(y, s, p.chips)
-            attend(p, r, a, step, 2 * yy + 1 - c, head)
-            tick()
-            if head == p.heads - 1:
+            attends(2 * yy + 1 - c, heads)
+            if final:
                 if s == 1:
                     out_ready()
                 shares.give(s, branch(2 * yy + 1 - c))
-            attend(p, r, a, step, 2 * yy + c, head)
-            tick()
-            if head == p.heads - 1:
+            attends(2 * yy + c, heads)
+            if final:
                 shares.pass_on(s, branch(2 * yy + c))
-        if head == p.heads - 1:
+        if final:
             after()
-        attend(p, r, a, step, 2 * y, head)
-        tick()
+        attends(2 * y, heads)
     shares.give(0, branch(2 * y + 1 - c))
     total = shares.total(branch(b))
     gather.end()
@@ -544,7 +553,7 @@
             r.dall[first : first + HD, pl.ds(start, QROWS)] = spread_rows(p, table, values, e).astype(BF)
 
 
-def attention_backward(p, r, a, step, state, grad, before, middle, head_done):
+def attention_backward(p, r, a, step, state, grad, passes, before, middle, head_done):
     b, _ = place()
     y, c = b // 2, lax.rem(b, 2)
     r.gt[b] = grad.T.astype(BF)
@@ -567,36 +576,38 @@
         return mm(r.all_w[:, : p.qkv], r.dall[:, lanes]) + mm(router_col, r.dlog[bb].astype(BF))
 
     shares = PackSum(p, r, a.back_sum_sems)
-    for head in range(p.heads):
-        if head == 0:
-            attention_grads(p, r, a, step, b)
-            gather.finish_near()
-            attention_grads(p, r, a, step, 2 * y + 1 - c)
-            attend_back(p, r, a, step, 2 * y, head)
-            gather.finish_far()
-            for s in range(1, p.chips):
-                each_block(lambda bb: attention_grads(p, r, a, step, bb), 2 * turn(y, s, p.chips), 2)
-            middle()
-        else:
-            attend_back(p, r, a, step, 2 * y, head)
+    def backs(bb, heads):
+        for head in heads:
+            attend_back(p, r, a, step, bb, head)
+
+    attention_grads(p, r, a, step, b)
+    gather.finish_near()
+    attention_grads(p, r, a, step, 2 * y + 1 - c)
+    backs(2 * y, range(p.heads))
+    gather.finish_far()
+    for s in range(1, p.chips):
+        each_block(lambda bb: attention_grads(p, r, a, step, bb), 2 * turn(y, s, p.chips), 2)
+    middle()
+    for heads in passes:
+        final = heads[-1] == p.heads - 1
         for s in range(1, p.chips):
-            each_block(lambda bb: attend_back(p, r, a, step, bb, head), 2 * turn(y, s, p.chips), 2)
-        if head == p.heads - 1:
+            each_block(lambda bb: backs(bb, heads), 2 * turn(y, s, p.chips), 2)
+        if final:
             for s in range(1, p.chips):
                 yy = turn(y, s, p.chips)
                 shares.give(s, branch(2 * yy + 1 - c))
                 shares.pass_on(s, branch(2 * yy + c))
-        attend_back(p, r, a, step, 2 * y + 1, head)
-        if head < p.heads - 1:
+        backs(2 * y + 1, heads)
+        if not final:
             key_value_grads(slice(0, p.length), slice(MAXLEN, MAXLEN + p.length))
-            head_done(head)
+            head_done(heads[-1])
     shares.give(0, branch(2 * y + 1 - c))
     own = branch(b)
     head_done(p.heads - 1)
     router = sum(mm_nt(r.dlog[bb].astype(BF), a.nt[bb]) for bb in range(p.blk))
     grad_n = shares.total(own).T
     gather.end()
-    back, gain = norm_back(state, r.gain_one[...].astype(F32), grad_n)
+    back, gain = norm_back(state, r.vectors[0:1, :].astype(F32), grad_n)
     return grad + back, gain, router
 
 
@@ -639,7 +650,7 @@
 
 
 def slot_groups(p):
-    per = max(1, p.experts // 4)
+    per = max(1, p.experts // (2 if p.slots <= 768 else 4))
     return [(pl.ds(first * p.cap, per * p.cap), range(first, first + per)) for first in range(0, p.experts, per)]
 
 
@@ -898,10 +909,10 @@
         saves.extend(moves(r, [(r.all_w, r.all_w_out), (r.disp, r.disp_out), (r.comb, r.comb_out)]))
         experts_pass()
 
-    total = attention_forward(p, r, r.a, 0, state, before, ready, tick, out_ready, after)
+    total = attention_forward(p, r, r.a, 0, state, by_head(p), before, ready, tick, out_ready, after)
     middle = state + total.T
     r.middle[...] = middle
-    m = (norm_parts(middle)[1] * r.gain_two[...].astype(F32)).astype(BF)
+    m = (norm_parts(middle)[1] * r.vectors[1:2, :].astype(F32)).astype(BF)
     r.outgoing[...] = mm(r.disp[0], m).astype(BF)
     there = slot_sends(p, r.outgoing, r.arrived, (r.go_s, r.go_r), slot_peer)
     saves.extend(moves(r, [(getattr(r.a, k), getattr(r, k + "_out")) for k in SAVED]))
@@ -944,7 +955,7 @@
     fill_router(p, r)
     weights = moves(r, [(r.all_in_in, r.all_in), (r.all_back_in, r.all_back)])
     first = r.first[...]
-    stop = 1.0 / (1.0 + jnp.exp(-jnp.sum(first * r.halt[...].astype(F32), axis=-1, keepdims=True)))
+    stop = 1.0 / (1.0 + jnp.exp(-jnp.sum(first * r.vectors[2:3, :].astype(F32), axis=-1, keepdims=True)))
     cot = r.cot[...].astype(F32)
     segment_columns(p, r.segments, r.seg_cols)
     answered(peers)
@@ -960,10 +971,10 @@
     def nothing(*_):
         pass
 
-    total = attention_forward(p, r, r.a, 1, first, before, nothing, nothing, nothing, nothing)
+    total = attention_forward(p, r, r.a, 1, first, [range(p.heads)], before, nothing, nothing, nothing, nothing)
     middle = first + total.T
     r.middle[...] = middle
-    m = (norm_parts(middle)[1] * r.gain_two[...].astype(F32)).astype(BF)
+    m = (norm_parts(middle)[1] * r.vectors[1:2, :].astype(F32)).astype(BF)
     r.outgoing[...] = mm(r.disp[...], m).astype(BF)
     there = slot_sends(p, r.outgoing, r.arrived, (r.go_s, r.go_r), slot_peer)
     transposed(r.wo, r.all_w, 0, p.qkv, p.all_cols, LANES)
@@ -989,7 +1000,7 @@
     saves.extend(moves(r, [(r.grad_in, r.grad_in_out), (r.grad_back, r.grad_back_out)]))
     attention_probs(p, r, r.a)
     receive(back, range(p.experts))
-    step_back, gain_two = norm_back(r.middle[...], r.gain_two[...].astype(F32), mm(r.comb[...], r.gret_in[...]))
+    step_back, gain_two = norm_back(r.middle[...], r.vectors[1:2, :].astype(F32), mm(r.comb[...], r.gret_in[...]))
     r.grad_gain_two[...] = gain_two
     grad_middle = (1.0 - stop) * cot + step_back
 
@@ -1003,7 +1014,7 @@
                 attention_weight_grads(p, r, r.a, part.start, part.stop, False)
 
     grad, gain_one, router = attention_backward(
-        p, r, r.a, 1, first, grad_middle, before_back, lambda: None, head_done
+        p, r, r.a, 1, first, grad_middle, [range(p.heads)], before_back, lambda: None, head_done
     )
     saves.extend(moves(r, [(r.grad_w, r.grad_w_out)]))
     r.grad_gain_one[...] = gain_one
@@ -1014,7 +1025,7 @@
     grad_stop = jnp.sum(cot * (first - second), axis=-1, keepdims=True)
     coeff = grad_stop * stop * (1.0 - stop)
     r.grad_halt[...] = jnp.sum(coeff * first, axis=0, keepdims=True)
-    r.grad_first[...] = stop * cot + coeff * r.halt[...].astype(F32) + grad
+    r.grad_first[...] = stop * cot + coeff * r.vectors[2:3, :].astype(F32) + grad
     for copies in (there, back, back_out):
         sent(copies)
     arrive(saves)
@@ -1089,7 +1100,7 @@
             )
     attention_probs(p, r, r.a)
     receive(back, range(p.experts))
-    step_back, gain_two = norm_back(r.middle[...], r.gain_two[...].astype(F32), mm(r.comb[...], r.gret_in[...]))
+    step_back, gain_two = norm_back(r.middle[...], r.vectors[1:2, :].astype(F32), mm(r.comb[...], r.gret_in[...]))
     grad_middle = grad_first + step_back
     wide, lo_copies, hi_copies = {}, {}, {}
 
@@ -1169,7 +1180,7 @@
         sum_pass(p.heads if head == 0 else head - 1)
 
     grad, gain_one, router = attention_backward(
-        p, r, r.a, 0, r.x[...].astype(F32), grad_middle, lambda: None, middle, head_done
+        p, r, r.a, 0, r.x[...].astype(F32), grad_middle, by_head(p), lambda: None, middle, head_done
     )
     small = r.out_small
     small[...] = jnp.zeros_like(small)
@@ -1357,9 +1368,7 @@
     cols, length, top = p.cols, p.length, p.top
     share, in_rows, back_rows = weight_key.shape[0], weight_in.shape[1], weight_back.shape[1]
 
-    gain_one = gain_mixer.reshape(1, width)
-    gain_two = gain_expert.reshape(1, width)
-    halt = halt_weight.reshape(1, width)
+    vectors = jnp.stack([gain_mixer, gain_expert, halt_weight])
     router_row, router = router_mixer.T, router_expert.T
 
     slots_bf = pltpu.VMEM((p.slots, width), BF)
@@ -1416,8 +1425,7 @@
             "segments": (segments, True),
             "attention_routes": (jnp.swapaxes(attention_routes[:, 0], 1, 2), True),
             "expert_routes": (jnp.swapaxes(expert_routes[:, 0], 1, 2), True),
-            "gain_one": (gain_one, True),
-            "gain_two": (gain_two, True),
+            "vectors": (vectors, True),
             "router_row": (router_row, True),
             "router_in": (router, True),
             "weight_query": (weight_query, True),
@@ -1472,11 +1480,9 @@
         {
             "first": (one.first, True),
             "cot": (cotangent[0], True),
-            "halt": (halt, True),
             "segments": (segments, True),
             "all_picks": (one.all_picks, True),
-            "gain_one": (gain_one, True),
-            "gain_two": (gain_two, True),
+            "vectors": (vectors, True),
             "router_row": (router_row, True),
             "router_in": (router, True),
             "disp_in": (one.disp_out, False),
@@ -1530,8 +1536,7 @@
             "middle": (one.middle, True),
             "segments": (segments, True),
             "all_picks": (one.all_picks, True),
-            "gain_one": (gain_one, True),
-            "gain_two": (gain_two, True),
+            "vectors": (vectors, True),
             "router_row": (router_row, True),
             "router_in": (router, True),
             "halt_before": (two.grad_halt, True),

time: 315 us -> 303 us (0.962)
  Pallas kernels: 306 us -> 294 us
    pallas_call x4, Pallas kernels: 306 us -> 294 us  [launch(): pl.pallas_call(kernel, out_shape=tuple((jax.ShapeDtypeStruct(shape, dtype...]
where the time goes in v1:
time: 303 us; the launch traced here: 297 us
  Pallas kernels  294 us (97%)
    pallas_call x4, Pallas kernels, launch(): pl.pallas_call(kernel, out_shape=tuple((jax.ShapeDtypeStruct(shape, dtype...  294 us

profile of v1, /device:TPU:0, one launch (start us, length us, event | category | flops | bytes accessed | tf_op | source)
XLA Modules:
  0.0 297.2 jit_solution(8371296896216816426)
XLA Ops:
  0.6 0.7 stack.14
  1.3 0.7 stack.13
  2.0 0.7 stack.12
  2.7 0.6 pad_maximum_fusion.refs_4_.refs_5_
  3.3 94.3 %forward.1 = (f32[256,512]{1,0:T(8,128)}, f32[256,512]{1,0:T(8,128)}, bf16[768,512]{1,0:T(8,128)(2,1)}, bf16[768,512]{1,0:T(8,128)(2,1)}, s32[4,16,256]{2,1,0:T(...) custom-call(bf16[256,512]{1,0:T(8,128)(2,1)} %bitcast.19, ...), custom_call_target="tpu_custom_call" | custom-call | tf_op jit(solution)/shard_map/forward/pallas_call | solution.py:1315
  97.6 96.6 %turn.1 = (bf16[256,512]{1,0:T(8,128)(2,1)}, f32[256,512]{1,0:T(8,128)}, f32[1,512]{1,0:T(1,128)}, f32[1,512]{1,0:T(1,128)}, f32[1,512]{1,0:T(1,128)}, /*index=5...) custom-call(f32[256,512]{1,0:T(8,128)} %get-tuple-element.60.refs_0_, ...), custom_call_target="tpu_custom_call" | custom-call | tf_op jit(solution)/shard_map/turn/pallas_call | solution.py:1315
  194.2 98.4 %backward.1 = (bf16[256,512]{1,0:T(8,128)(2,1)}, f32[64,2304]{1,0:T(8,128)}, bf16[2,128,2048]{2,1,0:T(8,128)(2,1)}, bf16[2,512,512]{2,1,0:T(8,128)(2,1)}, f32[32,512]{1,0:T(8,128)}) custom-call(bf16[256,512]{1,0:T(8,128)(2,1)} %bitcast.20, f32[256,512]{1,0:T(8,128)} %get-tuple-element.69.refs_1_, f32[256,512]{1,0:T(8,128)} %get-tuple-element.70.refs_2_, ...), custom_call_target="tpu_custom_call" | custom-call | tf_op jit(solution)/shard_map/backward/pallas_call | solution.py:1315
  292.6 4.4 %outputs.1 = (bf16[256,512]{1,0:T(8,128)(2,1)}, bf16[256,512]{1,0:T(8,128)(2,1)}, f32[8,64,128]{2,1,0:T(8,128)}, f32[64,128]{1,0:T(8,128)}, f32[64,128]{1,0:T(8,...) custom-call(bf16[256,512]{1,0:T(8,128)(2,1)} %get-tuple-element.68.r, ...), custom_call_target="tpu_custom_call" | custom-call | tf_op jit(solution)/shard_map/outputs/pallas_call | solution.py:1315
